TPU v7x, 512 devices: a whole 4x8x8 slice. The times are simulated.
512 devices in a mesh: section: 8 (over y), replica: 64 (over z, x, core).
Axes of the slice: x: 4, y: 8, z: 8, core: 2. Of those that a mesh axis runs over, the one named last changes fastest.
Arguments:
- coords_in: bfloat16 [2, 8192, 512], P(None, 'replica'), may hold values from -6 to 6
- token_rows: bfloat16 [2, 8192, 2048], P(None, 'replica'), may hold values from -16 to 16
- cotangent: bfloat16 [2, 8192, 512], P(None, 'replica'), may hold values from -6 to 6
- subspace_basis: bfloat16 [512, 2048], replicated, may hold values from -0.25 to 0.25
- norm_gain: float32 [8, 2048], P('section'), may hold values from 0.5 to 1.5
- gate_weight: float32 [8, 2048, 256], P('section', 'replica'), may hold values from -0.125 to 0.125
- up_weight: bfloat16 [8, 2048, 256], P('section', 'replica'), may hold values from -0.125 to 0.125
- down_weight: float32 [8, 256, 512], P('section', 'replica'), may hold values from -0.375 to 0.375
- gate_moment: float32 [8, 2048, 256], P('section', 'replica'), may hold values from -0.625 to 0.625
- gate_second: float32 [8, 2048, 256], P('section', 'replica'), may hold values from 0.01 to 0.1
- down_moment: float32 [8, 256, 512], P('section', 'replica'), may hold values from -0.625 to 0.625
- down_second: float32 [8, 256, 512], P('section', 'replica'), may hold values from 0.01 to 0.1
Outputs:
- section_coords: bfloat16 [8, 2, 8192, 512], P('section', None, 'replica')
- coord_grads: bfloat16 [8, 2, 8192, 512], P('section', None, 'replica')
- gate_new: float32 [8, 2048, 256], P('section', 'replica')
- gate_moment_new: float32 [8, 2048, 256], P('section', 'replica')
- gate_second_new: float32 [8, 2048, 256], P('section', 'replica')
- down_new: float32 [8, 256, 512], P('section', 'replica')
- down_moment_new: float32 [8, 256, 512], P('section', 'replica')
- down_second_new: float32 [8, 256, 512], P('section', 'replica')
All inputs are finite; a program needn't handle non-finite values.
Results may differ from a plain program's by a relative error of at most 0.03.
Values may be sent and summed in bfloat16 or wider, within the bound.
A program may use at most 64 MiB of HBM per device.

v0:
```python
import math
import jax
import jax.numpy as jnp
from jax import lax
from jax.sharding import PartitionSpec as P

epsilon = 1e-06
learn_rate = 0.001
decay_first = 0.9
decay_second = 0.95
step_count = 10
adam_floor = 1e-08


def from_behind(value, axis, steps):
    count = lax.axis_size(axis)
    first, last = (max(0, -steps), min(count, count - steps))
    return lax.ppermute(value, axis, [(source, source + steps) for source in range(first, last)])


def contract_last(left, right):
    return lax.dot_general(
        left, right, (((1,), (1,)), ((), ())), preferred_element_type=jnp.float32
    )


def contract_first(left, right):
    return lax.dot_general(
        left, right, (((0,), (0,)), ((), ())), preferred_element_type=jnp.float32
    )


def silu_parts(gate_value):
    sigma = jax.nn.sigmoid(gate_value)
    return (gate_value * sigma, sigma * (1.0 + gate_value * (1.0 - sigma)))


def section_forward(coords, token_block, subspace_basis, gain_row, w_gate, w_up, w_down):
    expanded = jnp.dot(
        coords, subspace_basis, preferred_element_type=jnp.float32
    ) + token_block.astype(jnp.float32)
    inverse = lax.rsqrt(jnp.mean(expanded * expanded, axis=1, keepdims=True) + epsilon)
    normed = (expanded * inverse * gain_row).astype(jnp.bfloat16)
    gate_value = jnp.dot(normed, w_gate, preferred_element_type=jnp.float32)
    up_value = jnp.dot(normed, w_up, preferred_element_type=jnp.float32)
    active, slope_value = silu_parts(gate_value)
    hidden = (active * up_value).astype(jnp.bfloat16)
    output = (
        coords.astype(jnp.float32) + jnp.dot(hidden, w_down, preferred_element_type=jnp.float32)
    ).astype(jnp.bfloat16)
    return (output, (expanded, inverse, normed, gate_value, up_value, hidden))


def section_backward(next_grad, saved, subspace_basis, gain_row, w_gate, w_up, w_down):
    expanded, inverse, normed, gate_value, up_value, hidden = saved
    hidden_grad = contract_last(next_grad, w_down)
    down_term = contract_first(hidden, next_grad)
    active, slope_value = silu_parts(gate_value)
    gate_grad = (hidden_grad * up_value * slope_value).astype(jnp.bfloat16)
    up_grad = (hidden_grad * active).astype(jnp.bfloat16)
    gate_term = contract_first(normed, gate_grad)
    normed_grad = contract_last(gate_grad, w_gate) + contract_last(up_grad, w_up)
    scaled = normed_grad * gain_row
    centred = expanded * inverse
    expanded_grad = (
        inverse * (scaled - centred * jnp.mean(scaled * centred, axis=1, keepdims=True))
    ).astype(jnp.bfloat16)
    coord_grad = (
        next_grad.astype(jnp.float32) + contract_last(expanded_grad, subspace_basis)
    ).astype(jnp.bfloat16)
    return (coord_grad, gate_term, down_term)


def adam_update(weight_now, moment, second, gradient):
    moment_new = decay_first * moment + (1.0 - decay_first) * gradient
    second_new = decay_second * second + (1.0 - decay_second) * gradient * gradient
    update = (
        learn_rate
        * (moment_new / (1.0 - decay_first**step_count))
        / (jnp.sqrt(second_new / (1.0 - decay_second**step_count)) + adam_floor)
    )
    return (weight_now - update, moment_new, second_new)


def per_device(
    coords_in,
    token_rows,
    cotangent,
    subspace_basis,
    norm_gain,
    gate_weight,
    up_weight,
    down_weight,
    gate_moment,
    gate_second,
    down_moment,
    down_second,
):
    batches = coords_in.shape[0]
    rows_dev = coords_in.shape[1]
    coord_width = subspace_basis.shape[0]
    model_width = subspace_basis.shape[1]
    sections = lax.axis_size("section")
    section_index = lax.axis_index("section")
    tick_count = sections + batches - 1
    w_gate, w_up, w_down = (
        lax.all_gather(gate_weight[0].astype(jnp.bfloat16), "replica", axis=0, tiled=True),
        lax.all_gather(up_weight[0], "replica", axis=0, tiled=True),
        lax.all_gather(down_weight[0].astype(jnp.bfloat16), "replica", axis=0, tiled=True),
    )
    hidden_width = w_gate.shape[1]
    weights = (subspace_basis, norm_gain, w_gate, w_up, w_down)
    kept_buffers = (jnp.zeros((batches, rows_dev, coord_width), jnp.bfloat16),)
    produced = jnp.zeros((batches, rows_dev, coord_width), jnp.bfloat16)
    blank = jnp.zeros((rows_dev, coord_width), jnp.bfloat16)

    def forward_tick(carry, tick_now):
        incoming, produced, kept_buffers = carry
        batch_now = tick_now - section_index
        is_live = (batch_now >= 0) & (batch_now < batches)
        slot_index = jnp.clip(batch_now, 0, batches - 1)
        source = jnp.where(
            section_index == 0, lax.dynamic_index_in_dim(coords_in, slot_index, 0, False), incoming
        )
        token_block = lax.dynamic_index_in_dim(token_rows, slot_index, 0, False)

        def forward_run_layer(buffers):
            produced_now, kept_now = buffers
            output, saved = section_forward(source, token_block, *weights)
            produced_now = lax.dynamic_update_index_in_dim(produced_now, output, slot_index, 0)
            entries = (source,)
            kept_now = tuple(
                (
                    lax.dynamic_update_index_in_dim(buffer, item, slot_index, 0)
                    for buffer, item in zip(kept_now, entries)
                )
            )
            return (produced_now, kept_now)

        produced, kept_buffers = lax.cond(
            is_live, forward_run_layer, lambda unchanged: unchanged, (produced, kept_buffers)
        )
        outgoing = lax.dynamic_index_in_dim(produced, slot_index, 0, False)
        incoming = from_behind(outgoing, "section", 1)
        return ((incoming, produced, kept_buffers), None)

    (incoming, produced, kept_buffers), unused = lax.scan(
        forward_tick, (blank, produced, kept_buffers), jnp.arange(tick_count, dtype=jnp.int32)
    )

    def backward_tick(carry, tick_now):
        incoming, returned, gate_acc, down_acc = carry
        batch_now = tick_now - (sections - 1 - section_index)
        is_live = (batch_now >= 0) & (batch_now < batches)
        slot_index = jnp.clip(batch_now, 0, batches - 1)
        next_grad = jnp.where(
            section_index == sections - 1,
            lax.dynamic_index_in_dim(cotangent, slot_index, 0, False),
            incoming,
        )

        def backward_run_layer(buffers):
            returned_now, gate_now, down_now = buffers
            source = lax.dynamic_index_in_dim(kept_buffers[0], slot_index, 0, False)
            token_block = lax.dynamic_index_in_dim(token_rows, slot_index, 0, False)
            saved = section_forward(source, token_block, *weights)[1]
            coord_grad, gate_term, down_term = section_backward(next_grad, saved, *weights)
            returned_now = lax.dynamic_update_index_in_dim(returned_now, coord_grad, slot_index, 0)
            return (returned_now, gate_now + gate_term, down_now + down_term)

        returned, gate_acc, down_acc = lax.cond(
            is_live, backward_run_layer, lambda unchanged: unchanged, (returned, gate_acc, down_acc)
        )
        outgoing = lax.dynamic_index_in_dim(returned, slot_index, 0, False)
        incoming = from_behind(outgoing, "section", -1)
        return ((incoming, returned, gate_acc, down_acc), None)

    returned = jnp.zeros((batches, rows_dev, coord_width), jnp.bfloat16)
    gate_zero = jnp.zeros((model_width, hidden_width), jnp.float32)
    down_zero = jnp.zeros((hidden_width, coord_width), jnp.float32)
    (incoming, returned, gate_acc, down_acc), unused = lax.scan(
        backward_tick,
        (blank, returned, gate_zero, down_zero),
        jnp.arange(tick_count, dtype=jnp.int32),
    )
    gate_share, down_share = (
        lax.psum_scatter(gate_acc, "replica", scatter_dimension=0, tiled=True),
        lax.psum_scatter(down_acc, "replica", scatter_dimension=0, tiled=True),
    )
    grad_scale = 1.0 / math.sqrt(batches * rows_dev * lax.axis_size("replica"))
    gate_new, gate_moment_new, gate_second_new = adam_update(
        gate_weight[0], gate_moment[0], gate_second[0], gate_share * grad_scale
    )
    down_new, down_moment_new, down_second_new = adam_update(
        down_weight[0], down_moment[0], down_second[0], down_share * grad_scale
    )
    return (
        produced[None],
        returned[None],
        gate_new[None],
        gate_moment_new[None],
        gate_second_new[None],
        down_new[None],
        down_moment_new[None],
        down_second_new[None],
    )


def solution(mesh):
    placed = (
        P(None, "replica", None),
        P(None, "replica", None),
        P(None, "replica", None),
        P(),
        P("section", None),
        P("section", "replica", None),
        P("section", "replica", None),
        P("section", "replica", None),
        P("section", "replica", None),
        P("section", "replica", None),
        P("section", "replica", None),
        P("section", "replica", None),
    )
    return jax.shard_map(
        per_device,
        mesh=mesh,
        in_specs=placed,
        out_specs=(
            P("section", None, "replica", None),
            P("section", None, "replica", None),
            P("section", "replica", None),
            P("section", "replica", None),
            P("section", "replica", None),
            P("section", "replica", None),
            P("section", "replica", None),
            P("section", "replica", None),
        ),
        check_vma=False,
    )
```

profile of v0, /device:TPU:8, one launch (start us, length us, event | category | flops | bytes accessed | tf_op | source)
XLA Modules:
  0.0 806.3 jit_solution(16639715585179184832)
XLA Ops:
  10.1 50.3 %all-gather.1 = bf16[64,4,512]{2,1,0:T(4,128)(2,1)S(1)} all-gather(bf16[1,4,512]{2,1,0:T(4,128)(2,1)S(1)} %fusion.30), channel_id=1, replica_groups=mesh['section'=8,'replica'=64] {'replica'}, dimensions={0}, use_global_device_ids=true | all-gather | bytes 266240 | tf_op jit(solution)/shard_map/all_gather | solution.py:109
  60.4 38.6 %all-gather.5.cloned.1.call-done = bf16[2048,256]{1,0:T(8,128)(2,1)} async-done(((bf16[32,256]{1,0:T(8,128)(2,1)}), bf16[2048,256]{1,0:T(8,128)(2,1)}) %all-gather.5.cloned.1.call-update) | async-done | bytes 1048592 | tf_op jit(solution)/shard_map/all_gather | solution.py:107
  99.0 83.1 %all-gather.7.cloned.1.call-done = bf16[1,2048,256]{2,1,0:T(8,128)(2,1)} async-done(((bf16[1,32,256]{2,1,0:T(8,128)(2,1)}), bf16[1,2048,256]{2,1,0:T(8,128)(2,1)}) %all-gather.7.cloned.1.call-update) | async-done | bytes 1048592 | tf_op jit(solution)/shard_map/all_gather | solution.py:108
  182.9 107.2 %while.33 = (s32[]{:T(128)}, bf16[128,512]{1,0:T(8,128)(2,1)S(1)}, bf16[2,128,512]{2,1,0:T(8,128)(2,1)}, bf16[2,128,512]{2,1,0:T(8,128)(2,1)S(1)}, s32[9]{0:T(12...) while((s32[]{:T(128)}, bf16[128,512]{1,0:T(8,128)(2,1)S(1)}, ...), condition=%wide.region_4.5_spmd, body=%wide.region_0.4_spmd.sunk | while | flops 573505664 | bytes 18533412 | solution.py:147
  188.5 7.3 collective-permute-done
  205.0 5.1 collective-permute-done
  211.3 5.0 conditional.4
  226.3 7.2 collective-permute-start
  247.3 6.9 collective-permute-start
  268.0 9.3 %collective-permute-start = (bf16[128,512]{1,0:T(8,128)(2,1)S(1)}, bf16[128,512]{1,0:T(8,128)(2,1)S(1)}, u32[]{:S(2)}, u32[]{:S(2)}) collective-permute-start(bf16[128,512]{1,0:T(8,128)(2,1)S(1)} %dynamic-slice_bitcast_fusion.4), channel_id=1, source_target_pairs={{0,64},{64,128},{128,192},{192,256},{256,320},{320,384},{384,448},... | collective-permute-start | bytes 393224 | tf_op jit(solution)/shard_map/while/body/eval_jaxpr/ppermute | solution.py:18
  282.0 5.6 collective-permute-start
  292.4 166.3 %while.34 = (s32[]{:T(128)}, bf16[128,512]{1,0:T(8,128)(2,1)S(1)}, bf16[2,128,512]{2,1,0:T(8,128)(2,1)}, f32[2048,256]{1,0:T(8,128)}, f32[256,512]{1,0:T(8,128)S...) while((s32[]{:T(128)}, bf16[128,512]{1,0:T(8,128)(2,1)S(1)}, ...), condition=%wide.region_10.11_spmd, body=%wide.region_5.10_spmd.sunk | while | flops 1281163392 | bytes 53303908 | solution.py:181
  296.5 6.7 collective-permute-done.1
  307.4 6.6 collective-permute-done.1
  318.1 8.6 %collective-permute-done.1 = bf16[128,512]{1,0:T(8,128)(2,1)S(1)} collective-permute-done((bf16[128,512]{1,0:T(8,128)(2,1)S(1)}, bf16[128,512]{1,0:T(8,128)(2,1)S(1)}, u32[]{:S(2)}, u32[]{:S(2)}) %collective-permute-start.1) | collective-permute-done | bytes 131104 | tf_op jit(solution)/shard_map/while/body/eval_jaxpr/ppermute | solution.py:18
  330.9 6.1 collective-permute-done.1
  341.2 5.2 collective-permute-done.1
  350.9 56.1 %collective-permute-done.1 = bf16[128,512]{1,0:T(8,128)(2,1)S(1)} collective-permute-done((bf16[128,512]{1,0:T(8,128)(2,1)S(1)}, bf16[128,512]{1,0:T(8,128)(2,1)S(1)}, u32[]{:S(2)}, u32[]{:S(2)}) %collective-permute-start.1) | collective-permute-done | bytes 131104 | tf_op jit(solution)/shard_map/while/body/eval_jaxpr/ppermute | solution.py:18
  408.2 8.6 %conditional.5 = ((bf16[2,128,512]{2,1,0:T(8,128)(2,1)}, f32[2048,256]{1,0:T(8,128)}, f32[256,512]{1,0:T(8,128)S(1)})) conditional(s32[]{:T(128)} %convert_element_type.126, (bf16[2,128,512]{2,1,0:T(8,128)(2,1)}, f32[2048,256]{1,0:T(8,128)}, f32[256,512]{1,0:T(8,128)S(1)}) %tuple.84, (pred[]{:T(512)}, bf16[2,128,512]{2,1,0:T(8,128)(2,1)}, s32[]{:T(128)}, ...), branch_computations={%region_6.6_spmd, %region_7.9_spmd} | conditional | flops 1281163392 | bytes 52517052 | solution.py:171
  419.7 6.1 collective-permute-done.1
  427.1 8.6 %conditional.5 = ((bf16[2,128,512]{2,1,0:T(8,128)(2,1)}, f32[2048,256]{1,0:T(8,128)}, f32[256,512]{1,0:T(8,128)S(1)})) conditional(s32[]{:T(128)} %convert_element_type.126, (bf16[2,128,512]{2,1,0:T(8,128)(2,1)}, f32[2048,256]{1,0:T(8,128)}, f32[256,512]{1,0:T(8,128)S(1)}) %tuple.84, (pred[]{:T(512)}, bf16[2,128,512]{2,1,0:T(8,128)(2,1)}, s32[]{:T(128)}, ...), branch_computations={%region_6.6_spmd, %region_7.9_spmd} | conditional | flops 1281163392 | bytes 52517052 | solution.py:171
  445.7 10.5 %collective-permute-start.1 = (bf16[128,512]{1,0:T(8,128)(2,1)S(1)}, bf16[128,512]{1,0:T(8,128)(2,1)S(1)}, u32[]{:S(2)}, u32[]{:S(2)}) collective-permute-start(bf16[128,512]{1,0:T(8,128)(2,1)S(1)} %dynamic-slice_bitcast_fusion.5), channel_id=1, source_target_pairs={{64,0},{128,64},{192,128},{256,192},{320,256},{384,320},{448,384},... | collective-permute-start | bytes 393224 | tf_op jit(solution)/shard_map/while/body/eval_jaxpr/ppermute | solution.py:18
  462.1 185.5 %all-reduce.3.cloned.1.call-done = f32[256,512]{1,0:T(8,128)} async-done(((f32[256,512]{1,0:T(8,128)}), f32[256,512]{1,0:T(8,128)}) %all-reduce.3.cloned.1.call-update) | async-done | bytes 524304
  648.9 149.5 %reduce-scatter.2.cloned.1.call-done = f32[32,256]{1,0:T(8,128)} async-done(((f32[2048,256]{1,0:T(8,128)}), f32[32,256]{1,0:T(8,128)}) %reduce-scatter.2.cloned.1.call-update) | async-done | bytes 32784 | tf_op jit(solution)/shard_map/reduce_scatter | solution.py:187
  (178 shorter events, 129.6 us)
Async XLA Ops:
  7.2 91.8 %all-gather.5.cloned.1.call-start = ((), (), s32[]{:S(2)}) async-start(), calls=%async_computation.1 | async-start | bytes 1064960 | tf_op jit(solution)/shard_map/all_gather | solution.py:107
  8.6 173.5 %all-gather.7.cloned.1.call-start = ((), (), s32[]{:S(2)}) async-start(), calls=%async_computation.3 | async-start | bytes 1064960 | tf_op jit(solution)/shard_map/all_gather | solution.py:108
  9.4 638.2 %all-reduce.3.cloned.1.call-start = ((), (), s32[]{:S(2)}) async-start(), calls=%async_computation.4 | async-start | bytes 1048576
  185.1 10.8 %collective-permute-start = (bf16[128,512]{1,0:T(8,128)(2,1)S(1)}, bf16[128,512]{1,0:T(8,128)(2,1)S(1)}, u32[]{:S(2)}, u32[]{:S(2)}) collective-permute-start(bf16[128,512]{1,0:T(8,128)(2,1)S(1)} %dynamic-slice_bitcast_fusion.4), channel_id=1, source_target_pairs={{0,64},{64,128},{128,192},{192,256},{256,320},{320,384},{384,448},... | collective-permute-start | bytes 393224 | tf_op jit(solution)/shard_map/while/body/eval_jaxpr/ppermute | solution.py:18
  203.0 7.1 collective-permute-start
  217.3 6.9 collective-permute-start
  226.3 9.7 %collective-permute-start = (bf16[128,512]{1,0:T(8,128)(2,1)S(1)}, bf16[128,512]{1,0:T(8,128)(2,1)S(1)}, u32[]{:S(2)}, u32[]{:S(2)}) collective-permute-start(bf16[128,512]{1,0:T(8,128)(2,1)S(1)} %dynamic-slice_bitcast_fusion.4), channel_id=1, source_target_pairs={{0,64},{64,128},{128,192},{192,256},{256,320},{320,384},{384,448},... | collective-permute-start | bytes 393224 | tf_op jit(solution)/shard_map/while/body/eval_jaxpr/ppermute | solution.py:18
  238.2 6.9 collective-permute-start
  247.3 9.4 %collective-permute-start = (bf16[128,512]{1,0:T(8,128)(2,1)S(1)}, bf16[128,512]{1,0:T(8,128)(2,1)S(1)}, u32[]{:S(2)}, u32[]{:S(2)}) collective-permute-start(bf16[128,512]{1,0:T(8,128)(2,1)S(1)} %dynamic-slice_bitcast_fusion.4), channel_id=1, source_target_pairs={{0,64},{64,128},{128,192},{192,256},{256,320},{320,384},{384,448},... | collective-permute-start | bytes 393224 | tf_op jit(solution)/shard_map/while/body/eval_jaxpr/ppermute | solution.py:18
  258.9 6.9 collective-permute-start
  268.0 11.9 %collective-permute-start = (bf16[128,512]{1,0:T(8,128)(2,1)S(1)}, bf16[128,512]{1,0:T(8,128)(2,1)S(1)}, u32[]{:S(2)}, u32[]{:S(2)}) collective-permute-start(bf16[128,512]{1,0:T(8,128)(2,1)S(1)} %dynamic-slice_bitcast_fusion.4), channel_id=1, source_target_pairs={{0,64},{64,128},{128,192},{192,256},{256,320},{320,384},{384,448},... | collective-permute-start | bytes 393224 | tf_op jit(solution)/shard_map/while/body/eval_jaxpr/ppermute | solution.py:18
  282.0 8.1 %collective-permute-start = (bf16[128,512]{1,0:T(8,128)(2,1)S(1)}, bf16[128,512]{1,0:T(8,128)(2,1)S(1)}, u32[]{:S(2)}, u32[]{:S(2)}) collective-permute-start(bf16[128,512]{1,0:T(8,128)(2,1)S(1)} %dynamic-slice_bitcast_fusion.4), channel_id=1, source_target_pairs={{0,64},{64,128},{128,192},{192,256},{256,320},{320,384},{384,448},... | collective-permute-start | bytes 393224 | tf_op jit(solution)/shard_map/while/body/eval_jaxpr/ppermute | solution.py:18
  294.6 8.7 %collective-permute-start.1 = (bf16[128,512]{1,0:T(8,128)(2,1)S(1)}, bf16[128,512]{1,0:T(8,128)(2,1)S(1)}, u32[]{:S(2)}, u32[]{:S(2)}) collective-permute-start(bf16[128,512]{1,0:T(8,128)(2,1)S(1)} %dynamic-slice_bitcast_fusion.5), channel_id=1, source_target_pairs={{64,0},{128,64},{192,128},{256,192},{320,256},{384,320},{448,384},... | collective-permute-start | bytes 393224 | tf_op jit(solution)/shard_map/while/body/eval_jaxpr/ppermute | solution.py:18
  305.4 8.6 %collective-permute-start.1 = (bf16[128,512]{1,0:T(8,128)(2,1)S(1)}, bf16[128,512]{1,0:T(8,128)(2,1)S(1)}, u32[]{:S(2)}, u32[]{:S(2)}) collective-permute-start(bf16[128,512]{1,0:T(8,128)(2,1)S(1)} %dynamic-slice_bitcast_fusion.5), channel_id=1, source_target_pairs={{64,0},{128,64},{192,128},{256,192},{320,256},{384,320},{448,384},... | collective-permute-start | bytes 393224 | tf_op jit(solution)/shard_map/while/body/eval_jaxpr/ppermute | solution.py:18
  316.2 10.6 %collective-permute-start.1 = (bf16[128,512]{1,0:T(8,128)(2,1)S(1)}, bf16[128,512]{1,0:T(8,128)(2,1)S(1)}, u32[]{:S(2)}, u32[]{:S(2)}) collective-permute-start(bf16[128,512]{1,0:T(8,128)(2,1)S(1)} %dynamic-slice_bitcast_fusion.5), channel_id=1, source_target_pairs={{64,0},{128,64},{192,128},{256,192},{320,256},{384,320},{448,384},... | collective-permute-start | bytes 393224 | tf_op jit(solution)/shard_map/while/body/eval_jaxpr/ppermute | solution.py:18
  329.0 8.1 %collective-permute-start.1 = (bf16[128,512]{1,0:T(8,128)(2,1)S(1)}, bf16[128,512]{1,0:T(8,128)(2,1)S(1)}, u32[]{:S(2)}, u32[]{:S(2)}) collective-permute-start(bf16[128,512]{1,0:T(8,128)(2,1)S(1)} %dynamic-slice_bitcast_fusion.5), channel_id=1, source_target_pairs={{64,0},{128,64},{192,128},{256,192},{320,256},{384,320},{448,384},... | collective-permute-start | bytes 393224 | tf_op jit(solution)/shard_map/while/body/eval_jaxpr/ppermute | solution.py:18
  339.2 7.1 collective-permute-start.1
  348.5 58.4 %collective-permute-start.1 = (bf16[128,512]{1,0:T(8,128)(2,1)S(1)}, bf16[128,512]{1,0:T(8,128)(2,1)S(1)}, u32[]{:S(2)}, u32[]{:S(2)}) collective-permute-start(bf16[128,512]{1,0:T(8,128)(2,1)S(1)} %dynamic-slice_bitcast_fusion.5), channel_id=1, source_target_pairs={{64,0},{128,64},{192,128},{256,192},{320,256},{384,320},{448,384},... | collective-permute-start | bytes 393224 | tf_op jit(solution)/shard_map/while/body/eval_jaxpr/ppermute | solution.py:18
  417.7 8.1 %collective-permute-start.1 = (bf16[128,512]{1,0:T(8,128)(2,1)S(1)}, bf16[128,512]{1,0:T(8,128)(2,1)S(1)}, u32[]{:S(2)}, u32[]{:S(2)}) collective-permute-start(bf16[128,512]{1,0:T(8,128)(2,1)S(1)} %dynamic-slice_bitcast_fusion.5), channel_id=1, source_target_pairs={{64,0},{128,64},{192,128},{256,192},{320,256},{384,320},{448,384},... | collective-permute-start | bytes 393224 | tf_op jit(solution)/shard_map/while/body/eval_jaxpr/ppermute | solution.py:18
  436.6 6.9 collective-permute-start.1
  445.7 13.0 %collective-permute-start.1 = (bf16[128,512]{1,0:T(8,128)(2,1)S(1)}, bf16[128,512]{1,0:T(8,128)(2,1)S(1)}, u32[]{:S(2)}, u32[]{:S(2)}) collective-permute-start(bf16[128,512]{1,0:T(8,128)(2,1)S(1)} %dynamic-slice_bitcast_fusion.5), channel_id=1, source_target_pairs={{64,0},{128,64},{192,128},{256,192},{320,256},{384,320},{448,384},... | collective-permute-start | bytes 393224 | tf_op jit(solution)/shard_map/while/body/eval_jaxpr/ppermute | solution.py:18
  458.7 339.6 %copy-start.10 = (f32[1,32,256]{2,1,0:T(8,128)S(1)}, f32[1,32,256]{2,1,0:T(8,128)}, u32[]{:S(2)}) copy-start(f32[1,32,256]{2,1,0:T(8,128)} %param.25) | copy-start | bytes 98308
  458.8 339.6 %copy-start.11 = (f32[1,32,256]{2,1,0:T(8,128)S(1)}, f32[1,32,256]{2,1,0:T(8,128)}, u32[]{:S(2)}) copy-start(f32[1,32,256]{2,1,0:T(8,128)} %param.29) | copy-start | bytes 98308
  459.5 338.8 %reduce-scatter.2.cloned.1.call-start = ((), (), s32[]{:S(2)}) async-start(), calls=%async_computation.2 | async-start | bytes 2129920 | tf_op jit(solution)/shard_map/reduce_scatter | solution.py:187
  (21 other events, 943.0 us)
Sparse Core Ops, SparseCore 0:
  11.9 87.0 all-gather.4
  102.3 79.7 all-gather.6
  459.7 187.8 all-reduce.2
  652.0 146.3 reduce-scatter.1
where the time goes:
time: 808 us; the launch traced here: 806 us
  waiting for transfers between devices  593 us (73%)
  starting transfers between devices  71.7 us (9%)
  blocking collectives  50.3 us (6%)
  local copies, waits for them, and re-layouts  35 us (4%)
  matrix products  19.5 us (2%)
  between operations  14.5 us (2%)
  loops' own time  13 us (2%)
  other arithmetic  9.4 us (1%)
    unnamed x5, waiting for transfers between devices  187 us
    reduce_scatter x1, waiting for transfers between devices, per_device(): lax.psum_scatter(gate_acc, 'replica', scatter_dimension=0, tiled=True)  149 us
    ppermute x18, waiting for transfers between devices, from_behind(): lax.ppermute(value, axis, [(source, source + steps) for source in range(f...  135 us
    all_gather x1, waiting for transfers between devices, per_device(): lax.all_gather(up_weight[0], 'replica', axis=0, tiled=True)  83.1 us
    ppermute x18, starting transfers between devices, from_behind(): lax.ppermute(value, axis, [(source, source + steps) for source in range(f...  71.6 us
    all_gather x1, blocking collectives, per_device(): lax.all_gather(down_weight[0].astype(jnp.bfloat16), 'replica', axis=0, ti...  50.3 us
    all_gather x1, waiting for transfers between devices, per_device(): lax.all_gather(gate_weight[0].astype(jnp.bfloat16), 'replica', axis=0, ti...  38.6 us
  transfers between devices with their start and end apart: 22, of which 22 were waited for; matrix products, arithmetic and copies ran while one was open for 0% of the time, Pallas kernels for 0%

commit v1 on v0

--- a/solution.py
+++ b/solution.py
@@ -10,6 +10,14 @@
 decay_second = 0.95
 step_count = 10
 adam_floor = 1e-08
+
+
+def gather_from_all(array, axis, dim):
+    length = lax.axis_size(axis)
+    repeats = [length if d == dim else 1 for d in range(array.ndim)]
+    return lax.all_to_all(
+        jnp.tile(array, repeats), axis, split_axis=dim, concat_axis=dim, tiled=True
+    )
 
 
 def from_behind(value, axis, steps):
@@ -104,7 +112,7 @@
     section_index = lax.axis_index("section")
     tick_count = sections + batches - 1
     w_gate, w_up, w_down = (
-        lax.all_gather(gate_weight[0].astype(jnp.bfloat16), "replica", axis=0, tiled=True),
+        gather_from_all(gate_weight[0].astype(jnp.bfloat16), "replica", 0),
         lax.all_gather(up_weight[0], "replica", axis=0, tiled=True),
         lax.all_gather(down_weight[0].astype(jnp.bfloat16), "replica", axis=0, tiled=True),
     )

time: 808 us -> 805 us (level)
  waiting for transfers between devices: 593 us -> 531 us
  starting transfers between devices: 71.7 us -> 100 us
  local copies, waits for them, and re-layouts: 35 us -> 48.4 us
  blocking collectives: 50.3 us -> 60.2 us
  matrix products: 19.5 us -> 28.2 us
    all_gather x1, waiting for transfers between devices: 83.1 us -> 26.6 us  [per_device(): lax.all_gather(up_weight[0], 'replica', axis=0, tiled=True)]
    all_gather x1 -> x0, waiting for transfers between devices: 38.6 us -> none  [per_device(): lax.all_gather(gate_weight[0].astype(jnp.bfloat16), 'replica', axis=0, ti...]
    ppermute x18, waiting for transfers between devices: 135 us -> 168 us  [from_behind(): lax.ppermute(value, axis, [(source, source + steps) for source in range(f...]
    ppermute x18, starting transfers between devices: 71.6 us -> 86.2 us  [from_behind(): lax.ppermute(value, axis, [(source, source + steps) for source in range(f...]
    all_to_all x0 -> x1, starting transfers between devices: none -> 14 us  [gather_from_all(): lax.all_to_all(jnp.tile(array, repeats), axis, split_axis=dim, concat_axi...]
    all_gather x1, blocking collectives: 50.3 us -> 60.2 us  [per_device(): lax.all_gather(down_weight[0].astype(jnp.bfloat16), 'replica', axis=0, ti...]
    unnamed x5 -> x4, waiting for transfers between devices: 187 us -> 186 us
  transfers between devices with their start and end apart: 22 -> 22, of which waited for: 22 -> 21; matrix products, arithmetic and copies ran while one was open for 0% -> 0% of each run, Pallas kernels for 0% -> 0%
where the time goes in v1:
time: 805 us; the launch traced here: 803 us
  waiting for transfers between devices  531 us (66%)
  starting transfers between devices  100 us (12%)
  blocking collectives  60.2 us (7%)
  local copies, waits for them, and re-layouts  48.4 us (6%)
  matrix products  28.2 us (4%)
  between operations  14.5 us (2%)
  loops' own time  12.9 us (2%)
    unnamed x4, waiting for transfers between devices  186 us
    ppermute x18, waiting for transfers between devices, from_behind(): lax.ppermute(value, axis, [(source, source + steps) for source in range(f...  168 us
    reduce_scatter x1, waiting for transfers between devices, per_device(): lax.psum_scatter(gate_acc, 'replica', scatter_dimension=0, tiled=True)  150 us
    ppermute x18, starting transfers between devices, from_behind(): lax.ppermute(value, axis, [(source, source + steps) for source in range(f...  86.2 us
    all_gather x1, blocking collectives, per_device(): lax.all_gather(down_weight[0].astype(jnp.bfloat16), 'replica', axis=0, ti...  60.2 us
    all_gather x1, waiting for transfers between devices, per_device(): lax.all_gather(up_weight[0], 'replica', axis=0, tiled=True)  26.6 us
  transfers between devices with their start and end apart: 22, of which 21 were waited for; matrix products, arithmetic and copies ran while one was open for 0% of the time, Pallas kernels for 0%

profile of v1, /device:TPU:8, one launch (start us, length us, event | category | flops | bytes accessed | tf_op | source)
XLA Modules:
  0.0 802.6 jit_solution(5700964105219359236)
XLA Ops:
  9.1 14.0 %all-to-all-start = ((bf16[64,32,256]{2,1,0:T(8,128)(2,1)}), bf16[64,32,256]{2,1,0:T(8,128)(2,1)}, u32[]{:S(2)}, u32[]{:S(2)}) async-start(bf16[64,32,256]{2,1,0:T(8,128)(2,1)} %tile.2), calls=%async_computation | async-start | bytes 2097152 | tf_op jit(solution)/shard_map/all_to_all | solution.py:18
  23.9 60.2 %all-gather.1 = bf16[64,4,512]{2,1,0:T(4,128)(2,1)S(1)} all-gather(bf16[1,4,512]{2,1,0:T(4,128)(2,1)S(1)} %fusion.30), channel_id=1, replica_groups=mesh['section'=8,'replica'=64] {'replica'}, dimensions={0}, use_global_device_ids=true | all-gather | bytes 266240 | tf_op jit(solution)/shard_map/all_gather | solution.py:117
  84.2 26.6 %all-gather.4.cloned.1.call-done = bf16[1,2048,256]{2,1,0:T(8,128)(2,1)} async-done(((bf16[1,32,256]{2,1,0:T(8,128)(2,1)}), bf16[1,2048,256]{2,1,0:T(8,128)(2,1)}) %all-gather.4.cloned.1.call-update) | async-done | bytes 1048592 | tf_op jit(solution)/shard_map/all_gather | solution.py:116
  112.3 130.7 %while.33 = (s32[]{:T(128)}, bf16[128,512]{1,0:T(8,128)(2,1)S(1)}, bf16[2,128,512]{2,1,0:T(8,128)(2,1)}, bf16[2,128,512]{2,1,0:T(8,128)(2,1)}, s32[9]{0:T(128)S(...) while((s32[]{:T(128)}, bf16[128,512]{1,0:T(8,128)(2,1)S(1)}, ...), condition=%wide.region_4.5_spmd, body=%wide.region_0.4_spmd.sunk | while | flops 573505664 | bytes 18501632 | solution.py:155
  117.9 11.3 %collective-permute-done = bf16[128,512]{1,0:T(8,128)(2,1)S(1)} collective-permute-done((bf16[128,512]{1,0:T(8,128)(2,1)S(1)}, bf16[128,512]{1,0:T(8,128)(2,1)S(1)}, u32[]{:S(2)}, u32[]{:S(2)}) %collective-permute-start) | collective-permute-done | bytes 131104 | tf_op jit(solution)/shard_map/while/body/eval_jaxpr/ppermute | solution.py:26
  130.4 8.9 %conditional.4 = ((bf16[2,128,512]{2,1,0:T(8,128)(2,1)}, bf16[2,128,512]{2,1,0:T(8,128)(2,1)})) conditional(s32[]{:T(128)} %convert_element_type.129, (bf16[2,128,512]{2,1,0:T(8,128)(2,1)}, bf16[2,128,512]{2,1,0:T(8,128)(2,1)}) %tuple.81, (pred[]{:T(512)}, bf16[2,128,512]{2,1,0:T(8,128)(2,1)}, s32[]{:T(128)}, bf16[128,512]{1,0:T(8,128)(2,1)S(1)}, ...), branch_computations={%region_1.1_spmd, %region_2.3_spmd} | conditional | flops 573505664 | bytes 17714814 | solution.py:148
  148.6 9.0 %conditional.4 = ((bf16[2,128,512]{2,1,0:T(8,128)(2,1)}, bf16[2,128,512]{2,1,0:T(8,128)(2,1)})) conditional(s32[]{:T(128)} %convert_element_type.129, (bf16[2,128,512]{2,1,0:T(8,128)(2,1)}, bf16[2,128,512]{2,1,0:T(8,128)(2,1)}) %tuple.81, (pred[]{:T(512)}, bf16[2,128,512]{2,1,0:T(8,128)(2,1)}, s32[]{:T(128)}, bf16[128,512]{1,0:T(8,128)(2,1)S(1)}, ...), branch_computations={%region_1.1_spmd, %region_2.3_spmd} | conditional | flops 573505664 | bytes 17714814 | solution.py:148
  167.5 11.1 %collective-permute-start = (bf16[128,512]{1,0:T(8,128)(2,1)S(1)}, bf16[128,512]{1,0:T(8,128)(2,1)S(1)}, u32[]{:S(2)}, u32[]{:S(2)}) collective-permute-start(bf16[128,512]{1,0:T(8,128)(2,1)S(1)} %dynamic-slice_bitcast_fusion.4), channel_id=1, source_target_pairs={{0,64},{64,128},{128,192},{192,256},{256,320},{320,384},{384,448},... | collective-permute-start | bytes 393224 | tf_op jit(solution)/shard_map/while/body/eval_jaxpr/ppermute | solution.py:26
  192.4 10.8 %collective-permute-start = (bf16[128,512]{1,0:T(8,128)(2,1)S(1)}, bf16[128,512]{1,0:T(8,128)(2,1)S(1)}, u32[]{:S(2)}, u32[]{:S(2)}) collective-permute-start(bf16[128,512]{1,0:T(8,128)(2,1)S(1)} %dynamic-slice_bitcast_fusion.4), channel_id=1, source_target_pairs={{0,64},{64,128},{128,192},{192,256},{256,320},{320,384},{384,448},... | collective-permute-start | bytes 393224 | tf_op jit(solution)/shard_map/while/body/eval_jaxpr/ppermute | solution.py:26
  217.0 13.2 %collective-permute-start = (bf16[128,512]{1,0:T(8,128)(2,1)S(1)}, bf16[128,512]{1,0:T(8,128)(2,1)S(1)}, u32[]{:S(2)}, u32[]{:S(2)}) collective-permute-start(bf16[128,512]{1,0:T(8,128)(2,1)S(1)} %dynamic-slice_bitcast_fusion.4), channel_id=1, source_target_pairs={{0,64},{64,128},{128,192},{192,256},{256,320},{320,384},{384,448},... | collective-permute-start | bytes 393224 | tf_op jit(solution)/shard_map/while/body/eval_jaxpr/ppermute | solution.py:26
  234.9 5.6 collective-permute-start
  246.1 210.0 %while.34 = (s32[]{:T(128)}, bf16[128,512]{1,0:T(8,128)(2,1)S(1)}, bf16[2,128,512]{2,1,0:T(8,128)(2,1)}, f32[2048,256]{1,0:T(8,128)}, f32[256,512]{1,0:T(8,128)}...) while((s32[]{:T(128)}, bf16[128,512]{1,0:T(8,128)(2,1)S(1)}, ...), condition=%wide.region_10.11_spmd, body=%wide.region_5.10_spmd.sunk | while | flops 1281163392 | bytes 52255420 | solution.py:189
  250.8 10.9 %collective-permute-done.1 = bf16[128,512]{1,0:T(8,128)(2,1)S(1)} collective-permute-done((bf16[128,512]{1,0:T(8,128)(2,1)}, bf16[128,512]{1,0:T(8,128)(2,1)S(1)}, u32[]{:S(2)}, u32[]{:S(2)}) %collective-permute-start.1) | collective-permute-done | bytes 131104 | tf_op jit(solution)/shard_map/while/body/eval_jaxpr/ppermute | solution.py:26
  266.5 6.8 collective-permute-done.1
  278.0 11.9 %collective-permute-done.1 = bf16[128,512]{1,0:T(8,128)(2,1)S(1)} collective-permute-done((bf16[128,512]{1,0:T(8,128)(2,1)}, bf16[128,512]{1,0:T(8,128)(2,1)S(1)}, u32[]{:S(2)}, u32[]{:S(2)}) %collective-permute-start.1) | collective-permute-done | bytes 131104 | tf_op jit(solution)/shard_map/while/body/eval_jaxpr/ppermute | solution.py:26
  294.7 5.3 collective-permute-done.1
  305.5 10.5 %collective-permute-done.1 = bf16[128,512]{1,0:T(8,128)(2,1)S(1)} collective-permute-done((bf16[128,512]{1,0:T(8,128)(2,1)}, bf16[128,512]{1,0:T(8,128)(2,1)S(1)}, u32[]{:S(2)}, u32[]{:S(2)}) %collective-permute-start.1) | collective-permute-done | bytes 131104 | tf_op jit(solution)/shard_map/while/body/eval_jaxpr/ppermute | solution.py:26
  320.8 72.8 %collective-permute-done.1 = bf16[128,512]{1,0:T(8,128)(2,1)S(1)} collective-permute-done((bf16[128,512]{1,0:T(8,128)(2,1)}, bf16[128,512]{1,0:T(8,128)(2,1)S(1)}, u32[]{:S(2)}, u32[]{:S(2)}) %collective-permute-start.1) | collective-permute-done | bytes 131104 | tf_op jit(solution)/shard_map/while/body/eval_jaxpr/ppermute | solution.py:26
  394.8 11.3 %conditional.5 = ((bf16[2,128,512]{2,1,0:T(8,128)(2,1)}, f32[2048,256]{1,0:T(8,128)}, f32[256,512]{1,0:T(8,128)})) conditional(s32[]{:T(128)} %convert_element_type.130, (bf16[2,128,512]{2,1,0:T(8,128)(2,1)}, f32[2048,256]{1,0:T(8,128)}, f32[256,512]{1,0:T(8,128)}) %tuple.84, (pred[]{:T(512)}, bf16[2,128,512]{2,1,0:T(8,128)(2,1)}, s32[]{:T(128)}, ...), branch_computations={%region_6.6_spmd, %region_7.9_spmd} | conditional | flops 1281163392 | bytes 51468560 | solution.py:179
  409.7 6.4 collective-permute-done.1
  417.3 11.3 %conditional.5 = ((bf16[2,128,512]{2,1,0:T(8,128)(2,1)}, f32[2048,256]{1,0:T(8,128)}, f32[256,512]{1,0:T(8,128)})) conditional(s32[]{:T(128)} %convert_element_type.130, (bf16[2,128,512]{2,1,0:T(8,128)(2,1)}, f32[2048,256]{1,0:T(8,128)}, f32[256,512]{1,0:T(8,128)}) %tuple.84, (pred[]{:T(512)}, bf16[2,128,512]{2,1,0:T(8,128)(2,1)}, s32[]{:T(128)}, ...), branch_computations={%region_6.6_spmd, %region_7.9_spmd} | conditional | flops 1281163392 | bytes 51468560 | solution.py:179
  440.1 13.2 %collective-permute-start.1 = (bf16[128,512]{1,0:T(8,128)(2,1)}, bf16[128,512]{1,0:T(8,128)(2,1)S(1)}, u32[]{:S(2)}, u32[]{:S(2)}) collective-permute-start(bf16[128,512]{1,0:T(8,128)(2,1)} %dynamic-slice_bitcast_fusion.5), channel_id=1, source_target_pairs={{64,0},{128,64},{192,128},{256,192},{320,256},{384,320},{448,384},... | collective-permute-start | bytes 393224 | tf_op jit(solution)/shard_map/while/body/eval_jaxpr/ppermute | solution.py:26
  458.8 184.9 %all-reduce.3.cloned.1.call-done = f32[256,512]{1,0:T(8,128)} async-done(((f32[256,512]{1,0:T(8,128)}), f32[256,512]{1,0:T(8,128)}) %all-reduce.3.cloned.1.call-update) | async-done | bytes 524304
  645.1 149.6 %reduce-scatter.2.cloned.1.call-done = f32[32,256]{1,0:T(8,128)} async-done(((f32[2048,256]{1,0:T(8,128)}), f32[32,256]{1,0:T(8,128)}) %reduce-scatter.2.cloned.1.call-update) | async-done | bytes 32784 | tf_op jit(solution)/shard_map/reduce_scatter | solution.py:195
  (188 shorter events, 150.5 us)
Async XLA Ops:
  9.1 75.2 %all-to-all-start = ((bf16[64,32,256]{2,1,0:T(8,128)(2,1)}), bf16[64,32,256]{2,1,0:T(8,128)(2,1)}, u32[]{:S(2)}, u32[]{:S(2)}) async-start(bf16[64,32,256]{2,1,0:T(8,128)(2,1)} %tile.2), calls=%async_computation | async-start | bytes 2097152 | tf_op jit(solution)/shard_map/all_to_all | solution.py:18
  23.1 87.7 %all-gather.4.cloned.1.call-start = ((), (), s32[]{:S(2)}) async-start(), calls=%async_computation.3 | async-start | bytes 1064960 | tf_op jit(solution)/shard_map/all_gather | solution.py:116
  23.8 619.8 %all-reduce.3.cloned.1.call-start = ((), (), s32[]{:S(2)}) async-start(), calls=%async_computation.4 | async-start | bytes 1048576
  114.5 14.7 %collective-permute-start = (bf16[128,512]{1,0:T(8,128)(2,1)S(1)}, bf16[128,512]{1,0:T(8,128)(2,1)S(1)}, u32[]{:S(2)}, u32[]{:S(2)}) collective-permute-start(bf16[128,512]{1,0:T(8,128)(2,1)S(1)} %dynamic-slice_bitcast_fusion.4), channel_id=1, source_target_pairs={{0,64},{64,128},{128,192},{192,256},{256,320},{320,384},{384,448},... | collective-permute-start | bytes 393224 | tf_op jit(solution)/shard_map/while/body/eval_jaxpr/ppermute | solution.py:26
  140.2 7.1 collective-permute-start
  158.4 6.9 collective-permute-start
  167.5 13.6 %collective-permute-start = (bf16[128,512]{1,0:T(8,128)(2,1)S(1)}, bf16[128,512]{1,0:T(8,128)(2,1)S(1)}, u32[]{:S(2)}, u32[]{:S(2)}) collective-permute-start(bf16[128,512]{1,0:T(8,128)(2,1)S(1)} %dynamic-slice_bitcast_fusion.4), channel_id=1, source_target_pairs={{0,64},{64,128},{128,192},{192,256},{256,320},{320,384},{384,448},... | collective-permute-start | bytes 393224 | tf_op jit(solution)/shard_map/while/body/eval_jaxpr/ppermute | solution.py:26
  183.3 6.9 collective-permute-start
  192.4 13.4 %collective-permute-start = (bf16[128,512]{1,0:T(8,128)(2,1)S(1)}, bf16[128,512]{1,0:T(8,128)(2,1)S(1)}, u32[]{:S(2)}, u32[]{:S(2)}) collective-permute-start(bf16[128,512]{1,0:T(8,128)(2,1)S(1)} %dynamic-slice_bitcast_fusion.4), channel_id=1, source_target_pairs={{0,64},{64,128},{128,192},{192,256},{256,320},{320,384},{384,448},... | collective-permute-start | bytes 393224 | tf_op jit(solution)/shard_map/while/body/eval_jaxpr/ppermute | solution.py:26
  207.9 6.9 collective-permute-start
  217.0 15.7 %collective-permute-start = (bf16[128,512]{1,0:T(8,128)(2,1)S(1)}, bf16[128,512]{1,0:T(8,128)(2,1)S(1)}, u32[]{:S(2)}, u32[]{:S(2)}) collective-permute-start(bf16[128,512]{1,0:T(8,128)(2,1)S(1)} %dynamic-slice_bitcast_fusion.4), channel_id=1, source_target_pairs={{0,64},{64,128},{128,192},{192,256},{256,320},{320,384},{384,448},... | collective-permute-start | bytes 393224 | tf_op jit(solution)/shard_map/while/body/eval_jaxpr/ppermute | solution.py:26
  234.9 8.1 %collective-permute-start = (bf16[128,512]{1,0:T(8,128)(2,1)S(1)}, bf16[128,512]{1,0:T(8,128)(2,1)S(1)}, u32[]{:S(2)}, u32[]{:S(2)}) collective-permute-start(bf16[128,512]{1,0:T(8,128)(2,1)S(1)} %dynamic-slice_bitcast_fusion.4), channel_id=1, source_target_pairs={{0,64},{64,128},{128,192},{192,256},{256,320},{320,384},{384,448},... | collective-permute-start | bytes 393224 | tf_op jit(solution)/shard_map/while/body/eval_jaxpr/ppermute | solution.py:26
  248.9 12.8 %collective-permute-start.1 = (bf16[128,512]{1,0:T(8,128)(2,1)}, bf16[128,512]{1,0:T(8,128)(2,1)S(1)}, u32[]{:S(2)}, u32[]{:S(2)}) collective-permute-start(bf16[128,512]{1,0:T(8,128)(2,1)} %dynamic-slice_bitcast_fusion.5), channel_id=1, source_target_pairs={{64,0},{128,64},{192,128},{256,192},{320,256},{384,320},{448,384},... | collective-permute-start | bytes 393224 | tf_op jit(solution)/shard_map/while/body/eval_jaxpr/ppermute | solution.py:26
  264.6 8.7 %collective-permute-start.1 = (bf16[128,512]{1,0:T(8,128)(2,1)}, bf16[128,512]{1,0:T(8,128)(2,1)S(1)}, u32[]{:S(2)}, u32[]{:S(2)}) collective-permute-start(bf16[128,512]{1,0:T(8,128)(2,1)} %dynamic-slice_bitcast_fusion.5), channel_id=1, source_target_pairs={{64,0},{128,64},{192,128},{256,192},{320,256},{384,320},{448,384},... | collective-permute-start | bytes 393224 | tf_op jit(solution)/shard_map/while/body/eval_jaxpr/ppermute | solution.py:26
  276.1 13.9 %collective-permute-start.1 = (bf16[128,512]{1,0:T(8,128)(2,1)}, bf16[128,512]{1,0:T(8,128)(2,1)S(1)}, u32[]{:S(2)}, u32[]{:S(2)}) collective-permute-start(bf16[128,512]{1,0:T(8,128)(2,1)} %dynamic-slice_bitcast_fusion.5), channel_id=1, source_target_pairs={{64,0},{128,64},{192,128},{256,192},{320,256},{384,320},{448,384},... | collective-permute-start | bytes 393224 | tf_op jit(solution)/shard_map/while/body/eval_jaxpr/ppermute | solution.py:26
  292.8 7.2 collective-permute-start.1
  302.8 13.2 %collective-permute-start.1 = (bf16[128,512]{1,0:T(8,128)(2,1)}, bf16[128,512]{1,0:T(8,128)(2,1)S(1)}, u32[]{:S(2)}, u32[]{:S(2)}) collective-permute-start(bf16[128,512]{1,0:T(8,128)(2,1)} %dynamic-slice_bitcast_fusion.5), channel_id=1, source_target_pairs={{64,0},{128,64},{192,128},{256,192},{320,256},{384,320},{448,384},... | collective-permute-start | bytes 393224 | tf_op jit(solution)/shard_map/while/body/eval_jaxpr/ppermute | solution.py:26
  318.9 74.7 %collective-permute-start.1 = (bf16[128,512]{1,0:T(8,128)(2,1)}, bf16[128,512]{1,0:T(8,128)(2,1)S(1)}, u32[]{:S(2)}, u32[]{:S(2)}) collective-permute-start(bf16[128,512]{1,0:T(8,128)(2,1)} %dynamic-slice_bitcast_fusion.5), channel_id=1, source_target_pairs={{64,0},{128,64},{192,128},{256,192},{320,256},{384,320},{448,384},... | collective-permute-start | bytes 393224 | tf_op jit(solution)/shard_map/while/body/eval_jaxpr/ppermute | solution.py:26
  407.7 8.3 %collective-permute-start.1 = (bf16[128,512]{1,0:T(8,128)(2,1)}, bf16[128,512]{1,0:T(8,128)(2,1)S(1)}, u32[]{:S(2)}, u32[]{:S(2)}) collective-permute-start(bf16[128,512]{1,0:T(8,128)(2,1)} %dynamic-slice_bitcast_fusion.5), channel_id=1, source_target_pairs={{64,0},{128,64},{192,128},{256,192},{320,256},{384,320},{448,384},... | collective-permute-start | bytes 393224 | tf_op jit(solution)/shard_map/while/body/eval_jaxpr/ppermute | solution.py:26
  430.2 7.1 collective-permute-start.1
  440.1 16.0 %collective-permute-start.1 = (bf16[128,512]{1,0:T(8,128)(2,1)}, bf16[128,512]{1,0:T(8,128)(2,1)S(1)}, u32[]{:S(2)}, u32[]{:S(2)}) collective-permute-start(bf16[128,512]{1,0:T(8,128)(2,1)} %dynamic-slice_bitcast_fusion.5), channel_id=1, source_target_pairs={{64,0},{128,64},{192,128},{256,192},{320,256},{384,320},{448,384},... | collective-permute-start | bytes 393224 | tf_op jit(solution)/shard_map/while/body/eval_jaxpr/ppermute | solution.py:26
  456.1 338.6 %copy-start.12 = (f32[1,32,256]{2,1,0:T(8,128)S(1)}, f32[1,32,256]{2,1,0:T(8,128)}, u32[]{:S(2)}) copy-start(f32[1,32,256]{2,1,0:T(8,128)} %param.25) | copy-start | bytes 98308
  456.1 338.6 %copy-start.13 = (f32[1,32,256]{2,1,0:T(8,128)S(1)}, f32[1,32,256]{2,1,0:T(8,128)}, u32[]{:S(2)}) copy-start(f32[1,32,256]{2,1,0:T(8,128)} %param.29) | copy-start | bytes 98308
  456.2 338.5 %reduce-scatter.2.cloned.1.call-start = ((), (), s32[]{:S(2)}) async-start(), calls=%async_computation.2 | async-start | bytes 2129920 | tf_op jit(solution)/shard_map/reduce_scatter | solution.py:195
  (26 other events, 1160.8 us)
Sparse Core Ops, SparseCore 0:
  27.3 83.4 all-gather.3
  456.3 187.3 all-reduce.2
  648.3 146.2 reduce-scatter.1
